TPU v7x, 32 devices: a whole 2x2x4 slice. The times are simulated.
32 devices in a mesh: head: 2 (over x), blk: 16 (over z, y, core).
Axes of the slice: x: 2, y: 2, z: 4, core: 2. Of those that a mesh axis runs over, the one named last changes fastest.
Arguments:
- hidden_in: bfloat16 [512, 2048], P('blk'), may hold values from -6 to 6
- attn_gain: float32 [2048], replicated, may hold values from 0.25 to 1.75
- w_query: bfloat16 [1536, 2048], P('head'), may hold values from -0.125 to 0.125
- w_latent: bfloat16 [576, 2048], P('head'), may hold values from -0.125 to 0.125
- kv_gain: float32 [512], replicated, may hold values from 0.25 to 1.75
- w_key_up: bfloat16 [512, 1024], P(None, 'head'), may hold values from -0.25 to 0.25
- w_value_up: bfloat16 [512, 1024], P(None, 'head'), may hold values from -0.25 to 0.25
- w_out: bfloat16 [1024, 2048], P('head'), may hold values from -0.1875 to 0.1875
- cache_rows: bfloat16 [6144, 576], P('blk'), may hold values from -6 to 6
- slot_request: int32 [48], P('blk'), may hold values from -1 to 15, as said below
- slot_block: int32 [48], P('blk'), may hold values from 0 to 16
- lengths: int32 [16], replicated, may hold values from 1 to 2176, as said below
- parents: int32 [16, 32], P('blk'), may hold values from -1 to 30, as said below
- accepted: int32 [16, 8], P('blk'), may hold values from 0 to 28, as said below
- new_slots: int32 [16, 8], P('blk'), may hold values from 0 to 255, as said below
- moe_gain: float32 [2048], replicated, may hold values from 0.25 to 1.75
- routes: int32 [512, 6], P('blk'), may hold values from 0 to 15, all different within a row; in each aligned block of 32 rows (0 to 31, 32 to 63, ...) at most 24 rows name the same one
- route_logits: float32 [512, 6], P('blk'), may hold values from -8 to 8
- w_gate: bfloat16 [16, 1408, 2048], P('blk', 'head'), may hold values from -0.125 to 0.125
- w_up: bfloat16 [16, 1408, 2048], P('blk', 'head'), may hold values from -0.125 to 0.125
- w_down: bfloat16 [16, 1408, 2048], P('blk', 'head'), may hold values from -0.15625 to 0.15625
Outputs:
- layer_out: bfloat16 [512, 2048], P('blk')
- new_rows: bfloat16 [256, 576], P('blk')
Inputs may be any that keep to these rules, and one draw needn't show every extreme that they name: A pool slot holds block slot_block of request slot_request or is free (-1); each request's blocks are distinct slots. Request r holds exactly ceil(lengths[r] / 128) pool blocks, numbered 0 upwards; one request holds 17 full blocks. `parents`: entry 0 of each request is -1 (the root); entry i names one of the tokens i - 4 .. i - 1. `accepted`: the first 8 tokens of a path from the root down the request's tree, root first. `new_slots`: all distinct. `routes`: within the 32 rows of one index of blk no expert is named more than 24 times.
All inputs are finite; a program needn't handle non-finite values.
Results may differ from a plain program's by a relative error of at most 0.0075.
Values may be sent and summed in bfloat16 or wider, within the bound.
No kernel may reach another device: no remote copies, remote signals or barrier semaphores. Data moves between devices by JAX's collectives and lax.ppermute only.
A program may use at most 128 MiB of HBM per device.

v0:
```python
import jax
import jax.numpy as jnp
from jax import lax
from jax.sharding import PartitionSpec as P

NOPE = 128
ROPE = 64
VDIM = 128
RANK = 512
NEW_DEV = 16
EPSILON = 1e-06
ROUTE_SCALE = 2.446
ROPE_BASE = 50000.0


def rms_scale(values, gain):
    values = values.astype(jnp.float32)
    mean_square = jnp.mean(values * values, axis=-1, keepdims=True)
    return values * lax.rsqrt(mean_square + EPSILON) * gain


def rotate(values, positions):
    width = values.shape[-1]
    half = width // 2
    freqs = ROPE_BASE ** (-2.0 * jnp.arange(half, dtype=jnp.float32) / width)
    angles = positions[:, None] * freqs[None, :]
    cosine = jnp.cos(angles)[:, None, :]
    sine = jnp.sin(angles)[:, None, :]
    first = values[..., :half]
    second = values[..., half:]
    return jnp.concatenate(
        [first * cosine - second * sine, second * cosine + first * sine], axis=-1
    )


def ancestry(parents):
    count = parents.shape[-1]
    nodes = jnp.arange(count, dtype=jnp.int32)
    reach = (parents[:, :, None] == nodes[None, None, :]).astype(jnp.float32) + jnp.eye(
        count, dtype=jnp.float32
    )[None]
    for level in range(count.bit_length()):
        reach = jnp.minimum(
            jnp.einsum("rij,rjk->rik", reach, reach, precision=lax.Precision.HIGHEST), 1.0
        )
    return reach


def expand(rows, key_up, value_up):
    count = rows.shape[0]
    heads_here = key_up.shape[1] // NOPE
    key_nope = (
        jnp.dot(rows[:, :RANK], key_up, preferred_element_type=jnp.float32)
        .astype(jnp.bfloat16)
        .reshape(count, heads_here, NOPE)
    )
    values = (
        jnp.dot(rows[:, :RANK], value_up, preferred_element_type=jnp.float32)
        .astype(jnp.bfloat16)
        .reshape(count, heads_here, VDIM)
    )
    shared = jnp.broadcast_to(rows[:, None, RANK:], (count, heads_here, ROPE))
    return (jnp.concatenate([key_nope, shared], axis=-1), values)


def project_rows(left, weight_rows):
    return lax.dot_general(
        left, weight_rows, (((1,), (1,)), ((), ())), preferred_element_type=jnp.float32
    )


def shards(
    hidden_in,
    attn_gain,
    w_query,
    w_latent,
    kv_gain,
    w_key_up,
    w_value_up,
    w_out,
    cache_rows,
    slot_request,
    slot_block,
    lengths,
    parents,
    accepted,
    new_slots,
    moe_gain,
    routes,
    route_logits,
    w_gate,
    w_up,
    w_down,
):
    block_count = lax.axis_size("blk")
    block_index = lax.axis_index("blk")
    tok_rows = hidden_in.shape[0]
    model_width = hidden_in.shape[1]
    req_local = parents.shape[0]
    draft_len = parents.shape[1]
    requests = lengths.shape[0]
    heads_here = w_key_up.shape[1] // NOPE
    top_count = routes.shape[1]
    scale = (NOPE + ROPE) ** (-0.5)
    normed = rms_scale(hidden_in, attn_gain).astype(jnp.bfloat16)
    reach = ancestry(parents)
    depth = jnp.sum(reach, axis=-1) - 1.0
    local_lengths = lax.dynamic_slice_in_dim(lengths, block_index * req_local, req_local, 0)
    positions = (local_lengths.astype(jnp.float32)[:, None] + depth).reshape(tok_rows)
    query_full = project_rows(normed, w_query).reshape(tok_rows, heads_here, NOPE + ROPE)
    queries = jnp.concatenate(
        [query_full[..., :NOPE], rotate(query_full[..., NOPE:], positions)], axis=-1
    ).astype(jnp.bfloat16)
    latent_part = project_rows(normed, w_latent)
    compressed = lax.all_gather(latent_part, "head", axis=1, tiled=True)
    draft_rows = jnp.concatenate(
        [
            rms_scale(compressed[:, :RANK], kv_gain),
            rotate(compressed[:, None, RANK:], positions)[:, 0],
        ],
        axis=-1,
    ).astype(jnp.bfloat16)
    chosen = (jnp.arange(req_local, dtype=jnp.int32)[:, None] * draft_len + accepted).reshape(-1)
    all_queries, all_chosen, all_targets = (
        lax.all_gather(
            queries.reshape(tok_rows, heads_here * (NOPE + ROPE)), "blk", axis=0, tiled=True
        ),
        lax.all_gather(draft_rows[chosen], "blk", axis=0, tiled=True),
        lax.all_gather(new_slots.reshape(-1), "blk", axis=0, tiled=True),
    )
    local_target = all_targets - block_index * NEW_DEV
    local_target = jnp.where((local_target >= 0) & (local_target < NEW_DEV), local_target, NEW_DEV)
    new_rows = (
        jnp.zeros((NEW_DEV, RANK + ROPE), jnp.bfloat16)
        .at[local_target]
        .set(all_chosen, mode="drop")
    )
    cache_keys, cache_values = expand(cache_rows, w_key_up, w_value_up)
    slot_count = slot_request.shape[0]
    block_len = cache_rows.shape[0] // slot_count
    owner = jnp.maximum(slot_request, 0)
    slot_queries = all_queries.reshape(requests, draft_len, heads_here, NOPE + ROPE)[owner]
    key_blocks = cache_keys.reshape(slot_count, block_len, heads_here, NOPE + ROPE)
    value_blocks = cache_values.reshape(slot_count, block_len, heads_here, VDIM)
    key_place = slot_block[:, None] * block_len + jnp.arange(block_len, dtype=jnp.int32)[None, :]
    live = (key_place < lengths[owner][:, None]) & (slot_request >= 0)[:, None]
    scores = (
        jnp.einsum("sqhd,skhd->sqhk", slot_queries, key_blocks, preferred_element_type=jnp.float32)
        * scale
    )
    weights = jnp.where(live[:, None, None, :], jnp.exp(scores), 0.0)
    slot_denom = jnp.sum(weights, axis=-1)
    slot_numer = jnp.einsum(
        "sqhk,skhv->sqhv",
        weights.astype(jnp.bfloat16),
        value_blocks,
        preferred_element_type=jnp.float32,
    )
    selector = (slot_request[None, :] == jnp.arange(requests, dtype=jnp.int32)[:, None]).astype(
        jnp.float32
    )
    numer_out = jnp.einsum(
        "rs,sqhv->rqhv", selector, slot_numer, precision=lax.Precision.HIGHEST
    ).reshape(requests * draft_len, heads_here * VDIM)
    denom_out = jnp.einsum(
        "rs,sqh->rqh", selector, slot_denom, precision=lax.Precision.HIGHEST
    ).reshape(requests * draft_len, heads_here)
    numer_in, denom_in = (
        lax.all_to_all(numer_out, "blk", split_axis=0, concat_axis=0, tiled=True),
        lax.all_to_all(denom_out, "blk", split_axis=0, concat_axis=0, tiled=True),
    )
    numer_far = numer_in.reshape(block_count, tok_rows, heads_here * VDIM).sum(axis=0)
    denom_far = denom_in.reshape(block_count, tok_rows, heads_here).sum(axis=0)
    draft_keys, draft_values = expand(draft_rows, w_key_up, w_value_up)
    own_keys = draft_keys.reshape(req_local, draft_len, heads_here, NOPE + ROPE)
    own_values = draft_values.reshape(req_local, draft_len, heads_here, VDIM)
    own_queries = queries.reshape(req_local, draft_len, heads_here, NOPE + ROPE)
    own_scores = (
        jnp.einsum("rqhd,rkhd->rqhk", own_queries, own_keys, preferred_element_type=jnp.float32)
        * scale
    )
    own_weights = jnp.where((reach > 0.5)[:, :, None, :], jnp.exp(own_scores), 0.0)
    denom = jnp.sum(own_weights, axis=-1).reshape(tok_rows, heads_here) + denom_far
    numer = jnp.einsum(
        "rqhk,rkhv->rqhv",
        own_weights.astype(jnp.bfloat16),
        own_values,
        preferred_element_type=jnp.float32,
    ).reshape(tok_rows, heads_here, VDIM)
    numer = numer + numer_far.reshape(tok_rows, heads_here, VDIM)
    attended = (numer / denom[..., None]).astype(jnp.bfloat16).reshape(tok_rows, heads_here * VDIM)
    attn_sum = lax.psum(jnp.dot(attended, w_out, preferred_element_type=jnp.float32), "head")
    resid = (hidden_in.astype(jnp.float32) + attn_sum).astype(jnp.bfloat16)
    moe_in = rms_scale(resid, moe_gain).astype(jnp.bfloat16)
    sigma = jax.nn.sigmoid(route_logits)
    route_weight = (ROUTE_SCALE * sigma / jnp.sum(sigma, axis=-1, keepdims=True)).reshape(-1)
    local_experts = w_gate.shape[0]
    expert_total = local_experts * block_count
    capacity = 2 * tok_rows * top_count // expert_total
    flat_routes = routes.reshape(-1)
    onehot = (flat_routes[:, None] == jnp.arange(expert_total, dtype=jnp.int32)[None, :]).astype(
        jnp.int32
    )
    rank = jnp.sum((jnp.cumsum(onehot, axis=0) - onehot) * onehot, axis=-1)
    slot_ids = flat_routes * capacity + rank
    source_rows = (
        jnp.full((expert_total * capacity,), tok_rows, jnp.int32)
        .at[slot_ids]
        .set(jnp.arange(tok_rows * top_count, dtype=jnp.int32) // top_count)
    )
    moe_pad = jnp.concatenate([moe_in, jnp.zeros((1, model_width), jnp.bfloat16)], axis=0)
    send_rows = moe_pad[source_rows]
    received = lax.all_to_all(send_rows, "blk", split_axis=0, concat_axis=0, tiled=True)
    grouped = received.reshape(block_count, local_experts, capacity, model_width)
    gate_val = jnp.einsum("sjcd,jfd->sjcf", grouped, w_gate, preferred_element_type=jnp.float32)
    up_val = jnp.einsum("sjcd,jfd->sjcf", grouped, w_up, preferred_element_type=jnp.float32)
    act = (jax.nn.silu(gate_val) * up_val).astype(jnp.bfloat16)
    expert_out = jnp.einsum(
        "sjcf,jfd->sjcd", act, w_down, preferred_element_type=jnp.float32
    ).reshape(block_count * local_experts * capacity, model_width)
    back = lax.all_to_all(expert_out, "blk", split_axis=0, concat_axis=0, tiled=True)
    routed_part = (
        (back[slot_ids] * route_weight[:, None])
        .reshape(tok_rows, top_count, model_width)
        .sum(axis=1)
    )
    routed = lax.psum(routed_part, "head")
    layer_out = (resid.astype(jnp.float32) + routed).astype(jnp.bfloat16)
    return (layer_out, new_rows)


def solution(mesh):
    return jax.shard_map(
        shards,
        mesh=mesh,
        in_specs=(
            P("blk", None),
            P(),
            P("head", None),
            P("head", None),
            P(),
            P(None, "head"),
            P(None, "head"),
            P("head", None),
            P("blk", None),
            P("blk"),
            P("blk"),
            P(),
            P("blk", None),
            P("blk", None),
            P("blk", None),
            P(),
            P("blk", None),
            P("blk", None),
            P("blk", "head", None),
            P("blk", "head", None),
            P("blk", "head", None),
        ),
        out_specs=(P("blk", None), P("blk", None)),
        check_vma=False,
    )
```

profile of v0, /device:TPU:0, one launch (start us, length us, event | category | flops | bytes accessed | tf_op | source)
XLA Modules:
  0.0 325.3 jit_solution(3864422452794586233)
XLA Ops:
  10.8 2.0 fusion.53
  17.2 1.4 copy_bitcast_fusion
  20.8 2.3 convolution_convert_fusion
  25.1 27.0 %all_gather.13 = bf16[512,768]{1,0:T(8,128)(2,1)} all-gather(bf16[32,768]{1,0:T(8,128)(2,1)} %convert_element_type.121), channel_id=1, replica_groups=mesh['head'=2,'blk'=16] {'blk'}, dimensions={0}, use_global_device_ids=true | all-gather | bytes 835584 | tf_op jit(solution)/shard_map/all_gather | solution.py:125
  52.2 3.4 %reshape.528 = bf16[16,32,4,192]{3,2,1,0:T(4,128)(2,1)} reshape(bf16[512,768]{1,0:T(8,128)(2,1)} %all_gather.13) | data formatting | bytes 1572864 | tf_op jit(solution)/shard_map/reshape | solution.py:142
  55.6 2.5 copy.84
  58.1 1.9 gather_fusion.1
  60.8 2.0 fusion.95
  63.8 3.5 %all-to-all-start.1 = ((f32[16,1,128]{2,1,0:T(1,128)}), f32[16,1,128]{2,1,0:T(1,128)S(1)}, u32[]{:S(2)}, u32[]{:S(2)}) async-start(f32[16,1,128]{2,1,0:T(1,128)} %reshape.622), calls=%async_computation.1 | async-start | bytes 16384 | tf_op jit(solution)/shard_map/all_to_all | solution.py:170
  69.5 1.7 convolution_bitcast_fusion.2
  71.2 4.8 %all-gather.2 = f32[2,288,32]{1,2,0:T(8,128)S(1)} all-gather(f32[1,288,32]{1,2,0:T(8,128)S(1)} %convolution_bitcast_fusion.2), channel_id=1, replica_groups=mesh['head'=2,'blk'=16] {'head'}, dimensions={0}, use_global_device_ids=true | all-gather | bytes 110592 | tf_op jit(solution)/shard_map/all_gather | solution.py:115
  76.3 2.3 convolution_convert_fusion.1
  78.6 1.9 reshape_reshape.4
  81.7 1.7 fusion.46
  85.1 2.7 copy.87
  87.8 2.6 all_to_all.22
  90.5 6.2 %all-to-all-start = ((f32[16,32,512]{2,1,0:T(8,128)}), f32[16,32,512]{2,1,0:T(8,128)}, u32[]{:S(2)}, u32[]{:S(2)}) async-start(f32[16,32,512]{2,1,0:T(8,128)} %all_to_all.22), calls=%async_computation | async-start | bytes 2097152 | tf_op jit(solution)/shard_map/all_to_all | solution.py:169
  105.3 14.4 %all-to-all-done = f32[16,32,512]{2,1,0:T(8,128)} async-done(((f32[16,32,512]{2,1,0:T(8,128)}), f32[16,32,512]{2,1,0:T(8,128)}, u32[]{:S(2)}, u32[]{:S(2)}) %all-to-all-start) | async-done | bytes 1048608 | tf_op jit(solution)/shard_map/all_to_all | solution.py:169
  121.1 2.8 fusion.56
  123.9 25.5 %all-reduce.6.cloned.1.call-done = f32[32,2048]{1,0:T(8,128)} async-done(((f32[32,2048]{1,0:T(8,128)}), f32[32,2048]{1,0:T(8,128)}) %all-reduce.6.cloned.1.call-update) | async-done | bytes 262160 | tf_op jit(solution)/shard_map/psum | solution.py:192
  150.6 3.1 gather_fusion.2
  153.8 42.0 %all_to_all.33 = bf16[16,24,2048]{2,1,0:T(8,128)(2,1)S(1)} all-to-all(bf16[16,24,2048]{2,1,0:T(8,128)(2,1)} %bitcast.171), channel_id=1, replica_groups=mesh['head'=2,'blk'=16] {'blk'}, dimensions={0} | all-to-all | bytes 3145728 | tf_op jit(solution)/shard_map/all_to_all | solution.py:213
  196.9 2.6 fusion.6
  199.4 8.3 %fusion = f32[16,24,2048]{2,1,0:T(8,128)} fusion(bf16[1,704,2048]{2,1,0:T(8,128)(2,1)} %param.41, bf16[16,24,2048]{2,1,0:T(8,128)(2,1)} %copy-done.3, bf16[1,704,2048]{2,1,0:T(8,128)(2,1)} %param.40, f32[16,1,24,704]{3,2,0,1:T(8,128)} %fusion.6), kind=kOutput, calls=%fused_computation.7 | convolution fusion | flops 2216214528 | bytes 11567104 | tf_op jit(solution)/shard_map/sjcf,jfd->sjcd/dot_general | solution.py:218
  207.7 5.2 %all-to-all-start.3 = ((f32[16,24,2048]{2,1,0:T(8,128)}), f32[16,24,2048]{2,1,0:T(8,128)}, u32[]{:S(2)}, u32[]{:S(2)}) async-start(f32[16,24,2048]{2,1,0:T(8,128)} %fusion), calls=%async_computation.3 | async-start | bytes 6291456 | tf_op jit(solution)/shard_map/all_to_all | solution.py:221
  215.2 69.5 %all-reduce.2 = s32[128]{0:T(128)S(1)} all-reduce(s32[128]{0:T(128)S(1)} %bitcast_dynamic-update-slice_fusion), channel_id=2, replica_groups=mesh['head'=2,'blk'=16] {'blk'}, use_global_device_ids=true, to_apply=%add.2 | all-reduce | flops 128 | bytes 1024
  284.7 4.9 %gather_fusion.3 = f32[192,2048]{1,0:T(8,128)} fusion(f32[384,2048]{1,0:T(8,128)} %bitcast.37, s32[1024]{0:T(1024)S(1)} %pad_clamp_fusion.1), kind=kCustom, calls=%fused_computation.3 | custom fusion | bytes 3146496 | tf_op jit(solution)/shard_map/gather | solution.py:223
  289.6 2.7 gather.21
  292.3 3.1 multiply_reduce_fusion
  295.3 19.8 %all-gather.1 = bf16[128,576]{1,0:T(8,128)(2,1)S(1)} all-gather(bf16[8,576]{1,0:T(8,128)(2,1)S(1)} %gather_fusion.4), channel_id=3, replica_groups=mesh['head'=2,'blk'=16] {'blk'}, dimensions={0}, use_global_device_ids=true | all-gather | bytes 156672 | tf_op jit(solution)/shard_map/all_gather | solution.py:128
  315.2 1.6 scatter_custom_fusion.1
  316.8 1.6 fusion.45
  (164 shorter events, 32.5 us)
Async XLA Ops:
  7.2 3.6 %copy-start = (bf16[768,2048]{1,0:T(8,128)(2,1)S(1)}, bf16[768,2048]{1,0:T(8,128)(2,1)}, u32[]{:S(2)}) copy-start(bf16[768,2048]{1,0:T(8,128)(2,1)} %param.23) | copy-start | bytes 9437188
  10.8 3.5 %copy-start.28 = (s32[3]{0:T(128)S(1)}, s32[3]{0:T(128)}, u32[]{:S(2)}) copy-start(s32[3]{0:T(128)} %param.31) | copy-start | bytes 40
  10.8 5.3 %copy-start.26 = (s32[1,32]{1,0:T(1,128)S(1)}, s32[1,32]{1,0:T(1,128)}, u32[]{:S(2)}) copy-start(s32[1,32]{1,0:T(1,128)} %param.33) | copy-start | bytes 388
  14.9 4.4 %copy-start.15 = (s32[1024]{0:T(1024)}, s32[1024]{0:T(1024)S(1)}, u32[]{:S(2)}) copy-start(s32[1024]{0:T(1024)S(1)} %pad_clamp_fusion.3) | copy-start | bytes 12292
  55.6 4.4 %copy-start.22 = (s32[3]{0:T(128)S(1)}, s32[3]{0:T(128)}, u32[]{:S(2)}) copy-start(s32[3]{0:T(128)} %gather_fusion) | copy-start | bytes 40
  55.6 5.2 %copy-start.6 = (bf16[3,128,64]{1,2,0:T(8,128)(2,1)S(1)}, bf16[3,128,64]{1,2,0:T(8,128)(2,1)}, u32[]{:S(2)}) copy-start(bf16[3,128,64]{1,2,0:T(8,128)(2,1)} %copy_bitcast_fusion) | copy-start | bytes 147460
  55.6 7.2 %copy-start.24 = (s32[3]{0:T(128)S(1)}, s32[3]{0:T(128)}, u32[]{:S(2)}) copy-start(s32[3]{0:T(128)} %param.30) | copy-start | bytes 40
  58.1 11.4 %copy-start.2 = (bf16[32,2048]{1,0:T(8,128)(2,1)S(1)}, bf16[32,2048]{1,0:T(8,128)(2,1)}, u32[]{:S(2)}) copy-start(bf16[32,2048]{1,0:T(8,128)(2,1)} %param.21) | copy-start | bytes 393220
  58.1 11.4 %copy-start.10 = (f32[2048]{0:T(1024)S(1)}, f32[2048]{0:T(1024)}, u32[]{:S(2)}) copy-start(f32[2048]{0:T(1024)} %param.22) | copy-start | bytes 24580
  63.8 26.7 %all-to-all-start.1 = ((f32[16,1,128]{2,1,0:T(1,128)}), f32[16,1,128]{2,1,0:T(1,128)S(1)}, u32[]{:S(2)}, u32[]{:S(2)}) async-start(f32[16,1,128]{2,1,0:T(1,128)} %reshape.622), calls=%async_computation.1 | async-start | bytes 16384 | tf_op jit(solution)/shard_map/all_to_all | solution.py:170
  68.8 9.8 %copy-start.13 = (s32[192]{0:T(256)}, s32[192]{0:T(256)S(1)}, u32[]{:S(2)}) copy-start(s32[192]{0:T(256)S(1)} %eq.99) | copy-start | bytes 2308
  76.2 4.3 %copy-start.7 = (bf16[3,32,4,128]{3,1,2,0:T(8,128)(2,1)S(1)}, bf16[3,32,4,128]{3,1,2,0:T(8,128)(2,1)}, u32[]{:S(2)}) copy-start(bf16[3,32,4,128]{3,1,2,0:T(8,128)(2,1)} %get-tuple-element.17) | copy-start | bytes 294916
  76.2 5.5 %copy-start.25 = (s32[3]{0:T(128)S(1)}, s32[3]{0:T(128)}, u32[]{:S(2)}) copy-start(s32[3]{0:T(128)} %param.30) | copy-start | bytes 40
  78.6 4.8 %copy-start.21 = (f32[512]{0:T(512)S(1)}, f32[512]{0:T(512)}, u32[]{:S(2)}) copy-start(f32[512]{0:T(512)} %param.25) | copy-start | bytes 6148
  85.1 5.3 %copy-start.20 = (s32[16,3]{0,1:T(4,128)}, s32[16,3]{0,1:T(4,128)S(1)}, u32[]{:S(2)}) copy-start(s32[16,3]{0,1:T(4,128)S(1)} %reduce-window.9) | copy-start | bytes 580
  90.4 7.5 %copy-start.17 = (f32[32]{0:T(128)S(1)}, f32[32]{0:T(128)}, u32[]{:S(2)}) copy-start(f32[32]{0:T(128)} %copy-done.16) | copy-start | bytes 388
  90.5 7.5 %copy-start.19 = (f32[32]{0:T(128)S(1)}, f32[32]{0:T(128)}, u32[]{:S(2)}) copy-start(f32[32]{0:T(128)} %copy-done.18) | copy-start | bytes 388
  90.5 9.0 %copy-start.5 = (bf16[32,4,192]{2,0,1:T(8,128)(2,1)S(1)}, bf16[32,4,192]{2,0,1:T(8,128)(2,1)}, u32[]{:S(2)}) copy-start(bf16[32,4,192]{2,0,1:T(8,128)(2,1)} %copy-done.4) | copy-start | bytes 147460
  90.5 7.8 %copy-start.11 = (f32[16,1,128]{2,1,0:T(1,128)}, f32[16,1,128]{2,1,0:T(1,128)S(1)}, u32[]{:S(2)}) copy-start(f32[16,1,128]{2,1,0:T(1,128)S(1)} %all-to-all-done.1) | copy-start | bytes 24580
  90.5 29.2 %all-to-all-start = ((f32[16,32,512]{2,1,0:T(8,128)}), f32[16,32,512]{2,1,0:T(8,128)}, u32[]{:S(2)}, u32[]{:S(2)}) async-start(f32[16,32,512]{2,1,0:T(8,128)} %all_to_all.22), calls=%async_computation | async-start | bytes 2097152 | tf_op jit(solution)/shard_map/all_to_all | solution.py:169
  96.7 52.7 %all-reduce.6.cloned.1.call-start = ((), (), s32[]{:S(2)}) async-start(), calls=%async_computation.4 | async-start | bytes 524288 | tf_op jit(solution)/shard_map/psum | solution.py:192
  96.7 3.9 %slice-start = ((s32[16,3]{0,1:T(4,128)}), s32[16,2]{0,1:T(2,128)S(1)}, s32[]{:S(2)}) async-start(s32[16,3]{0,1:T(4,128)} %copy-done.20), calls=%async_computation.6 | async-start | bytes 2048 | tf_op jit(solution)/shard_map/slice.1
  98.2 25.6 %copy-start.8 = (bf16[32,64]{1,0:T(8,128)(2,1)}, bf16[32,64]{1,0:T(8,128)(2,1)S(1)}, u32[]{:S(2)}) copy-start(bf16[32,64]{1,0:T(8,128)(2,1)S(1)} %maximum_bitcast_fusion) | copy-start | bytes 12292
  121.0 29.4 %copy-start.14 = (f32[2048]{0:T(1024)S(1)}, f32[2048]{0:T(1024)}, u32[]{:S(2)}) copy-start(f32[2048]{0:T(1024)} %param.36) | copy-start | bytes 24580
  153.8 43.1 %copy-start.27 = (bf16[1,704,2048]{2,1,0:T(8,128)(2,1)S(1)}, bf16[1,704,2048]{2,1,0:T(8,128)(2,1)}, u32[]{:S(2)}) copy-start(bf16[1,704,2048]{2,1,0:T(8,128)(2,1)} %param.39) | copy-start | bytes 8650756
  207.7 5.3 %copy-start.12 = (f32[32,6]{0,1:T(8,128)S(1)}, f32[32,6]{0,1:T(8,128)}, u32[]{:S(2)}) copy-start(f32[32,6]{0,1:T(8,128)} %param.38) | copy-start | bytes 2308
  207.7 5.4 %copy-start.31 = (u32[32]{0:T(128)S(1)}, u32[32]{0:T(128)}, u32[]{:S(2)}) copy-start(u32[32]{0:T(128)} %constant.93) | copy-start | bytes 388
  207.7 6.7 %copy-start.29 = (s32[1,8]{1,0:T(1,128)S(1)}, s32[1,8]{1,0:T(1,128)}, u32[]{:S(2)}) copy-start(s32[1,8]{1,0:T(1,128)} %param.34) | copy-start | bytes 100
  207.7 6.7 %copy-start.9 = (bf16[32,64]{1,0:T(8,128)(2,1)S(1)}, bf16[32,64]{1,0:T(8,128)(2,1)}, u32[]{:S(2)}) copy-start(bf16[32,64]{1,0:T(8,128)(2,1)} %copy-done.8) | copy-start | bytes 12292
  207.7 7.3 %copy-start.30 = (s32[1,8]{1,0:T(1,128)S(1)}, s32[1,8]{1,0:T(1,128)}, u32[]{:S(2)}) copy-start(s32[1,8]{1,0:T(1,128)} %param.35) | copy-start | bytes 100
  207.7 77.0 %all-to-all-start.3 = ((f32[16,24,2048]{2,1,0:T(8,128)}), f32[16,24,2048]{2,1,0:T(8,128)}, u32[]{:S(2)}, u32[]{:S(2)}) async-start(f32[16,24,2048]{2,1,0:T(8,128)} %fusion), calls=%async_computation.3 | async-start | bytes 6291456 | tf_op jit(solution)/shard_map/all_to_all | solution.py:221
  213.0 103.8 %all-reduce.8.cloned.1.call-start = ((), (), s32[]{:S(2)}) async-start(), calls=%async_computation.5 | async-start | bytes 524288 | tf_op jit(solution)/shard_map/psum | solution.py:227
  (6 other events, 5.8 us)
Sparse Core Ops, SparseCore 0:
  124.0 25.3 all-reduce.5
  295.5 21.2 all-reduce.7
where the time goes:
time: 327 us; the launch traced here: 325 us
  blocking collectives  163 us (50%)
  local copies, waits for them, and re-layouts  43.3 us (13%)
  waiting for transfers between devices  39.9 us (12%)
  matrix products  31.6 us (10%)
  other arithmetic  16.5 us (5%)
  between operations  15.9 us (5%)
  starting transfers between devices  14.9 us (5%)
    unnamed x1, blocking collectives  69.5 us
    all_to_all x1, blocking collectives, shards(): lax.all_to_all(send_rows, 'blk', split_axis=0, concat_axis=0, tiled=True)  42 us
    all_gather x1, blocking collectives, shards(): lax.all_gather(queries.reshape(tok_rows, heads_here * (NOPE + ROPE)), 'bl...  27 us
    psum x1, waiting for transfers between devices, shards(): lax.psum(jnp.dot(attended, w_out, preferred_element_type=jnp.float32), 'h...  25.5 us
    all_gather x1, blocking collectives, shards(): lax.all_gather(draft_rows[chosen], 'blk', axis=0, tiled=True)  19.8 us
    all_to_all x1, waiting for transfers between devices, shards(): lax.all_to_all(numer_out, 'blk', split_axis=0, concat_axis=0, tiled=True)  14.4 us
    dot_general x1, matrix products, shards(): jnp.einsum('sjcf,jfd->sjcd', act, w_down, preferred_element_type=jnp.floa...  8.28 us
    gather x2, local copies, waits for them, and re-layouts, shards(): back[slot_ids] * route_weight[:, None]  7.57 us
  transfers between devices with their start and end apart: 5, of which 2 were waited for; matrix products, arithmetic and copies ran while one was open for 8% of the time, Pallas kernels for 0%

commit v1 on v0

--- a/solution.py
+++ b/solution.py
@@ -189,7 +189,9 @@
     ).reshape(tok_rows, heads_here, VDIM)
     numer = numer + numer_far.reshape(tok_rows, heads_here, VDIM)
     attended = (numer / denom[..., None]).astype(jnp.bfloat16).reshape(tok_rows, heads_here * VDIM)
-    attn_sum = lax.psum(jnp.dot(attended, w_out, preferred_element_type=jnp.float32), "head")
+    attn_sum = jnp.sum(
+        lax.all_gather(jnp.dot(attended, w_out, preferred_element_type=jnp.float32), "head"), axis=0
+    )
     resid = (hidden_in.astype(jnp.float32) + attn_sum).astype(jnp.bfloat16)
     moe_in = rms_scale(resid, moe_gain).astype(jnp.bfloat16)
     sigma = jax.nn.sigmoid(route_logits)

time: 327 us -> 313 us (0.957)
  waiting for transfers between devices: 39.9 us -> 18 us
  blocking collectives: 163 us -> 174 us
    psum x1 -> x0, waiting for transfers between devices: 25.5 us -> none  [shards(): lax.psum(jnp.dot(attended, w_out, preferred_element_type=jnp.float32), 'h...]
    all_gather x0 -> x1, blocking collectives: none -> 9.73 us  [shards(): lax.all_gather(jnp.dot(attended, w_out, preferred_element_type=jnp.float3...]
  transfers between devices with their start and end apart: 5 -> 4, of which waited for: 2 -> 2; matrix products, arithmetic and copies ran while one was open for 8% -> 8% of each run, Pallas kernels for 0% -> 0%
where the time goes in v1:
time: 313 us; the launch traced here: 312 us
  blocking collectives  174 us (56%)
  local copies, waits for them, and re-layouts  42.2 us (13%)
  matrix products  30.3 us (10%)
  waiting for transfers between devices  18 us (6%)
  other arithmetic  17 us (5%)
  between operations  15.9 us (5%)
  starting transfers between devices  14.9 us (5%)
    unnamed x1, blocking collectives  69.5 us
    all_to_all x1, blocking collectives, shards(): lax.all_to_all(send_rows, 'blk', split_axis=0, concat_axis=0, tiled=True)  42.9 us
    all_gather x1, blocking collectives, shards(): lax.all_gather(queries.reshape(tok_rows, heads_here * (NOPE + ROPE)), 'bl...  27 us
    all_gather x1, blocking collectives, shards(): lax.all_gather(draft_rows[chosen], 'blk', axis=0, tiled=True)  19.8 us
    all_to_all x1, waiting for transfers between devices, shards(): lax.all_to_all(numer_out, 'blk', split_axis=0, concat_axis=0, tiled=True)  17.1 us
    all_gather x1, blocking collectives, shards(): lax.all_gather(jnp.dot(attended, w_out, preferred_element_type=jnp.float3...  9.73 us
    dot_general x1, matrix products, shards(): jnp.einsum('sjcf,jfd->sjcd', act, w_down, preferred_element_type=jnp.floa...  8.3 us
    gather x2, local copies, waits for them, and re-layouts, shards(): back[slot_ids] * route_weight[:, None]  7.57 us
  transfers between devices with their start and end apart: 4, of which 2 were waited for; matrix products, arithmetic and copies ran while one was open for 8% of the time, Pallas kernels for 0%

profile of v1, /device:TPU:0, one launch (start us, length us, event | category | flops | bytes accessed | tf_op | source)
XLA Modules:
  0.0 311.9 jit_solution(7981610280791947897)
XLA Ops:
  10.8 2.0 fusion.53
  20.8 2.3 convolution_convert_fusion
  25.1 27.0 %all_gather.19 = bf16[512,768]{1,0:T(8,128)(2,1)} all-gather(bf16[32,768]{1,0:T(8,128)(2,1)} %convert_element_type.121), channel_id=1, replica_groups=mesh['head'=2,'blk'=16] {'blk'}, dimensions={0}, use_global_device_ids=true | all-gather | bytes 835584 | tf_op jit(solution)/shard_map/all_gather | solution.py:125
  52.2 3.4 %reshape.528 = bf16[16,32,4,192]{3,2,1,0:T(4,128)(2,1)} reshape(bf16[512,768]{1,0:T(8,128)(2,1)} %all_gather.19) | data formatting | bytes 1572864 | tf_op jit(solution)/shard_map/reshape | solution.py:142
  55.6 2.5 copy.84
  58.1 1.9 gather_fusion.1
  60.8 2.0 fusion.95
  63.8 3.5 %all-to-all-start.1 = ((f32[16,1,128]{2,1,0:T(1,128)}), f32[16,1,128]{2,1,0:T(1,128)S(1)}, u32[]{:S(2)}, u32[]{:S(2)}) async-start(f32[16,1,128]{2,1,0:T(1,128)} %reshape.623), calls=%async_computation.1 | async-start | bytes 16384 | tf_op jit(solution)/shard_map/all_to_all | solution.py:170
  68.7 1.7 convolution_bitcast_fusion.2
  70.5 4.8 %all-gather.3 = f32[2,288,32]{1,2,0:T(8,128)S(1)} all-gather(f32[1,288,32]{1,2,0:T(8,128)S(1)} %convolution_bitcast_fusion.2), channel_id=1, replica_groups=mesh['head'=2,'blk'=16] {'head'}, dimensions={0}, use_global_device_ids=true | all-gather | bytes 110592 | tf_op jit(solution)/shard_map/all_gather | solution.py:115
  77.1 2.3 convolution_convert_fusion.1
  79.4 1.8 reshape_reshape.4
  82.5 1.7 fusion.46
  84.8 2.7 copy.87
  87.5 2.6 all_to_all.22
  90.1 6.2 %all-to-all-start = ((f32[16,32,512]{2,1,0:T(8,128)}), f32[16,32,512]{2,1,0:T(8,128)}, u32[]{:S(2)}, u32[]{:S(2)}) async-start(f32[16,32,512]{2,1,0:T(8,128)} %all_to_all.22), calls=%async_computation | async-start | bytes 2097152 | tf_op jit(solution)/shard_map/all_to_all | solution.py:169
  102.2 17.1 %all-to-all-done = f32[16,32,512]{2,1,0:T(8,128)} async-done(((f32[16,32,512]{2,1,0:T(8,128)}), f32[16,32,512]{2,1,0:T(8,128)}, u32[]{:S(2)}, u32[]{:S(2)}) %all-to-all-start) | async-done | bytes 1048608 | tf_op jit(solution)/shard_map/all_to_all | solution.py:169
  120.7 2.0 fusion.56
  122.7 9.7 %all-gather = f32[64,2048]{1,0:T(8,128)} all-gather(f32[32,2048]{1,0:T(8,128)S(1)} %fusion.56), channel_id=2, replica_groups=mesh['head'=2,'blk'=16] {'head'}, dimensions={0}, use_global_device_ids=true | all-gather | bytes 786432 | tf_op jit(solution)/shard_map/all_gather | solution.py:193
  132.5 1.8 reduce_sum.117
  135.5 3.1 %gather_fusion.2 = bf16[384,2048]{1,0:T(8,128)(2,1)} fusion(bf16[33,2048]{1,0:T(8,128)(2,1)S(1)} %concatenate.30, s32[1024]{0:T(1024)S(1)} %pad_clamp_fusion.2), kind=kCustom, calls=%fused_computation.2 | custom fusion | bytes 3147264 | tf_op jit(solution)/shard_map/gather | solution.py:214
  138.6 42.9 %all_to_all.33 = bf16[16,24,2048]{2,1,0:T(8,128)(2,1)S(1)} all-to-all(bf16[16,24,2048]{2,1,0:T(8,128)(2,1)} %bitcast.172), channel_id=1, replica_groups=mesh['head'=2,'blk'=16] {'blk'}, dimensions={0} | all-to-all | bytes 3145728 | tf_op jit(solution)/shard_map/all_to_all | solution.py:215
  182.7 2.6 fusion.6
  185.2 8.3 %fusion = f32[16,24,2048]{2,1,0:T(8,128)} fusion(bf16[1,704,2048]{2,1,0:T(8,128)(2,1)} %param.41, bf16[16,24,2048]{2,1,0:T(8,128)(2,1)} %copy-done.3, bf16[1,704,2048]{2,1,0:T(8,128)(2,1)} %param.40, f32[16,1,24,704]{3,2,0,1:T(8,128)} %fusion.6), kind=kOutput, calls=%fused_computation.7 | convolution fusion | flops 2216214528 | bytes 11567104 | tf_op jit(solution)/shard_map/sjcf,jfd->sjcd/dot_general | solution.py:220
  193.5 5.2 %all-to-all-start.3 = ((f32[16,24,2048]{2,1,0:T(8,128)}), f32[16,24,2048]{2,1,0:T(8,128)}, u32[]{:S(2)}, u32[]{:S(2)}) async-start(f32[16,24,2048]{2,1,0:T(8,128)} %fusion), calls=%async_computation.3 | async-start | bytes 6291456 | tf_op jit(solution)/shard_map/all_to_all | solution.py:223
  201.0 69.5 %all-reduce.2 = s32[128]{0:T(128)S(1)} all-reduce(s32[128]{0:T(128)S(1)} %bitcast_dynamic-update-slice_fusion), channel_id=3, replica_groups=mesh['head'=2,'blk'=16] {'blk'}, use_global_device_ids=true, to_apply=%add.2 | all-reduce | flops 128 | bytes 1024
  270.5 4.9 %gather_fusion.3 = f32[192,2048]{1,0:T(8,128)} fusion(f32[384,2048]{1,0:T(8,128)} %bitcast.38, s32[1024]{0:T(1024)S(1)} %pad_clamp_fusion.1), kind=kCustom, calls=%fused_computation.3 | custom fusion | bytes 3146496 | tf_op jit(solution)/shard_map/gather | solution.py:225
  275.4 2.7 gather.21
  278.1 3.1 multiply_reduce_fusion
  281.2 19.8 %all-gather.2 = bf16[128,576]{1,0:T(8,128)(2,1)S(1)} all-gather(bf16[8,576]{1,0:T(8,128)(2,1)S(1)} %gather_fusion.4), channel_id=4, replica_groups=mesh['head'=2,'blk'=16] {'blk'}, dimensions={0}, use_global_device_ids=true | all-gather | bytes 156672 | tf_op jit(solution)/shard_map/all_gather | solution.py:128
  301.0 1.6 scatter_custom_fusion.1
  303.5 1.6 fusion.45
  (152 shorter events, 31.6 us)
Async XLA Ops:
  7.2 3.6 %copy-start = (bf16[768,2048]{1,0:T(8,128)(2,1)S(1)}, bf16[768,2048]{1,0:T(8,128)(2,1)}, u32[]{:S(2)}) copy-start(bf16[768,2048]{1,0:T(8,128)(2,1)} %param.23) | copy-start | bytes 9437188
  10.2 0.6 copy-start.18
  10.8 2.3 copy-start.1
  10.8 3.5 %copy-start.23 = (s32[3]{0:T(128)S(1)}, s32[3]{0:T(128)}, u32[]{:S(2)}) copy-start(s32[3]{0:T(128)} %param.31) | copy-start | bytes 40
  10.8 5.3 %copy-start.21 = (s32[1,32]{1,0:T(1,128)S(1)}, s32[1,32]{1,0:T(1,128)}, u32[]{:S(2)}) copy-start(s32[1,32]{1,0:T(1,128)} %param.33) | copy-start | bytes 388
  14.9 4.4 %copy-start.11 = (s32[1024]{0:T(1024)}, s32[1024]{0:T(1024)S(1)}, u32[]{:S(2)}) copy-start(s32[1024]{0:T(1024)S(1)} %pad_clamp_fusion.3) | copy-start | bytes 12292
  18.7 0.6 copy-start.12
  18.7 0.6 copy-start.14
  19.4 0.6 copy-start.4
  55.6 4.4 %copy-start.17 = (s32[3]{0:T(128)S(1)}, s32[3]{0:T(128)}, u32[]{:S(2)}) copy-start(s32[3]{0:T(128)} %gather_fusion) | copy-start | bytes 40
  55.6 5.2 %copy-start.6 = (bf16[3,128,64]{1,2,0:T(8,128)(2,1)S(1)}, bf16[3,128,64]{1,2,0:T(8,128)(2,1)}, u32[]{:S(2)}) copy-start(bf16[3,128,64]{1,2,0:T(8,128)(2,1)} %copy_bitcast_fusion) | copy-start | bytes 147460
  55.6 7.2 %copy-start.19 = (s32[3]{0:T(128)S(1)}, s32[3]{0:T(128)}, u32[]{:S(2)}) copy-start(s32[3]{0:T(128)} %param.30) | copy-start | bytes 40
  58.1 10.7 %copy-start.2 = (bf16[32,2048]{1,0:T(8,128)(2,1)S(1)}, bf16[32,2048]{1,0:T(8,128)(2,1)}, u32[]{:S(2)}) copy-start(bf16[32,2048]{1,0:T(8,128)(2,1)} %param.21) | copy-start | bytes 393220
  58.1 10.7 %copy-start.7 = (f32[2048]{0:T(1024)S(1)}, f32[2048]{0:T(1024)}, u32[]{:S(2)}) copy-start(f32[2048]{0:T(1024)} %param.22) | copy-start | bytes 24580
  60.8 14.9 %copy-start.16 = (f32[512]{0:T(512)S(1)}, f32[512]{0:T(512)}, u32[]{:S(2)}) copy-start(f32[512]{0:T(512)} %param.25) | copy-start | bytes 6148
  63.8 26.3 %all-to-all-start.1 = ((f32[16,1,128]{2,1,0:T(1,128)}), f32[16,1,128]{2,1,0:T(1,128)S(1)}, u32[]{:S(2)}, u32[]{:S(2)}) async-start(f32[16,1,128]{2,1,0:T(1,128)} %reshape.623), calls=%async_computation.1 | async-start | bytes 16384 | tf_op jit(solution)/shard_map/all_to_all | solution.py:170
  77.0 5.4 %copy-start.20 = (s32[3]{0:T(128)S(1)}, s32[3]{0:T(128)}, u32[]{:S(2)}) copy-start(s32[3]{0:T(128)} %param.30) | copy-start | bytes 40
  90.1 6.7 %copy-start.13 = (f32[32]{0:T(128)S(1)}, f32[32]{0:T(128)}, u32[]{:S(2)}) copy-start(f32[32]{0:T(128)} %copy-done.12) | copy-start | bytes 388
  90.1 6.7 %copy-start.15 = (f32[32]{0:T(128)S(1)}, f32[32]{0:T(128)}, u32[]{:S(2)}) copy-start(f32[32]{0:T(128)} %copy-done.14) | copy-start | bytes 388
  90.1 8.2 %copy-start.5 = (bf16[32,4,192]{2,0,1:T(8,128)(2,1)S(1)}, bf16[32,4,192]{2,0,1:T(8,128)(2,1)}, u32[]{:S(2)}) copy-start(bf16[32,4,192]{2,0,1:T(8,128)(2,1)} %copy-done.4) | copy-start | bytes 147460
  90.1 8.4 %copy-start.8 = (f32[16,1,128]{2,1,0:T(1,128)}, f32[16,1,128]{2,1,0:T(1,128)S(1)}, u32[]{:S(2)}) copy-start(f32[16,1,128]{2,1,0:T(1,128)S(1)} %all-to-all-done.1) | copy-start | bytes 24580
  90.1 29.2 %all-to-all-start = ((f32[16,32,512]{2,1,0:T(8,128)}), f32[16,32,512]{2,1,0:T(8,128)}, u32[]{:S(2)}, u32[]{:S(2)}) async-start(f32[16,32,512]{2,1,0:T(8,128)} %all_to_all.22), calls=%async_computation | async-start | bytes 2097152 | tf_op jit(solution)/shard_map/all_to_all | solution.py:169
  122.7 12.6 %copy-start.10 = (f32[2048]{0:T(1024)S(1)}, f32[2048]{0:T(1024)}, u32[]{:S(2)}) copy-start(f32[2048]{0:T(1024)} %param.36) | copy-start | bytes 24580
  138.6 44.0 %copy-start.22 = (bf16[1,704,2048]{2,1,0:T(8,128)(2,1)S(1)}, bf16[1,704,2048]{2,1,0:T(8,128)(2,1)}, u32[]{:S(2)}) copy-start(bf16[1,704,2048]{2,1,0:T(8,128)(2,1)} %param.39) | copy-start | bytes 8650756
  181.5 1.1 copy-start.3
  193.5 5.3 %copy-start.9 = (f32[32,6]{0,1:T(8,128)S(1)}, f32[32,6]{0,1:T(8,128)}, u32[]{:S(2)}) copy-start(f32[32,6]{0,1:T(8,128)} %param.38) | copy-start | bytes 2308
  193.5 5.4 %copy-start.26 = (u32[32]{0:T(128)S(1)}, u32[32]{0:T(128)}, u32[]{:S(2)}) copy-start(u32[32]{0:T(128)} %constant.93) | copy-start | bytes 388
  193.5 6.7 %copy-start.24 = (s32[1,8]{1,0:T(1,128)S(1)}, s32[1,8]{1,0:T(1,128)}, u32[]{:S(2)}) copy-start(s32[1,8]{1,0:T(1,128)} %param.34) | copy-start | bytes 100
  193.5 7.3 %copy-start.25 = (s32[1,8]{1,0:T(1,128)S(1)}, s32[1,8]{1,0:T(1,128)}, u32[]{:S(2)}) copy-start(s32[1,8]{1,0:T(1,128)} %param.35) | copy-start | bytes 100
  193.5 77.0 %all-to-all-start.3 = ((f32[16,24,2048]{2,1,0:T(8,128)}), f32[16,24,2048]{2,1,0:T(8,128)}, u32[]{:S(2)}, u32[]{:S(2)}) async-start(f32[16,24,2048]{2,1,0:T(8,128)} %fusion), calls=%async_computation.3 | async-start | bytes 6291456 | tf_op jit(solution)/shard_map/all_to_all | solution.py:223
  198.8 104.7 %all-reduce.5.cloned.1.call-start = ((), (), s32[]{:S(2)}) async-start(), calls=%async_computation.4 | async-start | bytes 524288 | tf_op jit(solution)/shard_map/psum | solution.py:229
Sparse Core Ops, SparseCore 0:
  281.3 22.1 all-reduce.4
